TPU v7x, 32 devices: a whole 2x2x4 slice. The times are simulated.
32 devices in a mesh: dp: 8 (over y, x, core), tensor: 4 (over z).
Axes of the slice: x: 2, y: 2, z: 4, core: 2. Of those that a mesh axis runs over, the one named last changes fastest.
Arguments:
- hidden: bfloat16 [2048, 4608], P('dp', 'tensor'), may hold values from -0.890625 to 0.890625
- out_grad: bfloat16 [2048, 2304], P('dp'), may hold values from -1.1875 to 1.1875
- weight: bfloat16 [4608, 2304], P('tensor'), may hold values from -0.09375 to 0.09375
- first_moment: float32 [2304, 4608], P('dp', 'tensor'), may hold values from -3 to 3
- second_moment: float32 [2304, 4608], P('dp', 'tensor'), may hold values from 0.1 to 4
- next_hidden: bfloat16 [2048, 4608], P('dp', 'tensor'), may hold values from -6 to 6
Outputs:
- input_grad: bfloat16 [2048, 4608], P('dp', 'tensor')
- first_new: float32 [2304, 4608], P('dp', 'tensor')
- second_new: float32 [2304, 4608], P('dp', 'tensor')
- new_weight: bfloat16 [2304, 4608], P('dp', 'tensor')
- next_out: bfloat16 [2048, 2304], P('dp')
All inputs are finite; a program needn't handle non-finite values.
Results may differ from a plain program's by a relative error of at most 0.007.
Values may be sent and summed in bfloat16 or wider, within the bound.
A program may use at most 128 MiB of HBM per device.

v0:
```python
import jax
import jax.numpy as jnp
from jax import lax
from jax.sharding import PartitionSpec as P

beta_first = 0.9
beta_second = 0.95
learn_rate = 0.001
weight_decay = 0.1
epsilon = 1e-08
correct_first = 0.999973438601112
correct_second = 0.99407947077967


def tensor_total(partial_value):
    result = lax.psum(partial_value, "tensor").astype(jnp.bfloat16)
    return result


def shards(hidden, out_grad, weight, first_moment, second_moment, next_hidden):
    columns = first_moment.shape[0]
    position = lax.axis_index("dp") * columns
    input_grad = lax.dot_general(
        out_grad, weight, (((1,), (1,)), ((), ())), preferred_element_type=jnp.float32
    ).astype(jnp.bfloat16)
    grad = lax.psum_scatter(
        lax.dot_general(
            out_grad, hidden, (((0,), (0,)), ((), ())), preferred_element_type=jnp.float32
        ).astype(jnp.bfloat16),
        "dp",
        scatter_dimension=0,
        tiled=True,
    ).astype(jnp.float32)
    first_new = beta_first * first_moment + (1.0 - beta_first) * grad
    second_new = beta_second * second_moment + (1.0 - beta_second) * grad * grad
    current = lax.dynamic_slice_in_dim(weight, position, columns, 1).astype(jnp.float32).T
    update = first_new / correct_first / (jnp.sqrt(second_new / correct_second) + epsilon)
    new_weight = (current - learn_rate * (update + weight_decay * current)).astype(jnp.bfloat16)
    partial_value = lax.dot_general(
        next_hidden,
        lax.all_gather(new_weight, "dp", axis=0, tiled=True),
        (((1,), (1,)), ((), ())),
        preferred_element_type=jnp.float32,
    )
    next_out = tensor_total(partial_value)
    return (input_grad, first_new, second_new, new_weight, next_out)


def solution(mesh):
    placed = (
        P("dp", "tensor"),
        P("dp", None),
        P("tensor", None),
        P("dp", "tensor"),
        P("dp", "tensor"),
        P("dp", "tensor"),
    )
    return jax.shard_map(
        shards,
        mesh=mesh,
        in_specs=placed,
        out_specs=(
            P("dp", "tensor"),
            P("dp", "tensor"),
            P("dp", "tensor"),
            P("dp", "tensor"),
            P("dp", None),
        ),
        check_vma=False,
    )
```

profile of v0, /device:TPU:0, one launch (start us, length us, event | category | flops | bytes accessed | tf_op | source)
XLA Modules:
  0.0 221.1 jit_solution(10383142957821425002)
XLA Ops:
  7.2 0.0 copy-start
  7.2 0.0 reduce-scatter.2.cloned.1.call-start
  7.2 1.2 copy-done
  8.4 5.1 %convolution_convert_fusion = bf16[2304,1152]{1,0:T(8,128)(2,1)} fusion(bf16[256,2304]{1,0:T(8,128)(2,1)S(1)} %copy-done, bf16[256,1152]{1,0:T(8,128)(2,1)} %param.6), kind=kOutput, calls=%fused_computation | convolution fusion | flops 1361608704 | bytes 7077888 | tf_op jit(solution)/shard_map/dot_general | solution.py:27
  13.6 0.0 reduce-scatter.2.cloned.1.call-update
  13.6 0.0 all-gather.2.cloned.1.call-start
  13.6 1.6 constant_dynamic-slice_fusion
  15.3 0.4 copy.13
  15.7 57.7 %reduce-scatter.2.cloned.1.call-done = bf16[288,1152]{1,0:T(8,128)(2,1)} async-done(((bf16[2304,1152]{1,0:T(8,128)(2,1)}), bf16[288,1152]{1,0:T(8,128)(2,1)}) %reduce-scatter.2.cloned.1.call-update) | async-done | bytes 663568 | tf_op jit(solution)/shard_map/reduce_scatter | solution.py:26
  73.4 4.4 %fusion.4 = (bf16[288,1152]{1,0:T(8,128)(2,1)}, f32[288,1152]{1,0:T(8,128)}, f32[288,1152]{1,0:T(8,128)}) fusion(bf16[1152,288]{0,1:T(8,128)(2,1)S(1)} %copy.13, bf16[288,1152]{1,0:T(8,128)(2,1)} %reduce-scatter.2.cloned.1.call-done, f32[288,1152]{1,0:T(8,128)} %param.10, f32[288,1152]{1,0:T(8,128)} %param.9), kind=kLoop, calls=%fused_computation.11 | loop fusion | flops 5971968 | bytes 7299072 | tf_op jit(solution)/shard_map/convert_element_type | solution.py:38
  77.7 0.0 all-gather.2.cloned.1.call-update
  77.8 0.0 copy-start.1
  77.8 5.1 %convolution_convert_fusion.1 = bf16[256,1152]{1,0:T(8,128)(2,1)} fusion(bf16[256,2304]{1,0:T(8,128)(2,1)S(1)} %copy-done, bf16[1152,2304]{1,0:T(8,128)(2,1)} %param.8), kind=kOutput, calls=%fused_computation.2 | convolution fusion | flops 1359249408 | bytes 7077888 | tf_op jit(solution)/shard_map/dot_general | solution.py:23
  82.9 36.4 %all-gather.2.cloned.1.call-done = bf16[2304,1152]{1,0:T(8,128)(2,1)} async-done(((bf16[288,1152]{1,0:T(8,128)(2,1)}), bf16[2304,1152]{1,0:T(8,128)(2,1)}) %all-gather.2.cloned.1.call-update) | async-done | bytes 5308432 | tf_op jit(solution)/shard_map/all_gather | solution.py:41
  119.3 0.0 copy-done.1
  119.3 5.7 %convolution_bitcast_fusion = f32[256,2304]{0,1:T(8,128)} fusion(bf16[2304,1152]{1,0:T(8,128)(2,1)} %all-gather.2.cloned.1.call-done, bf16[256,1152]{1,0:T(8,128)(2,1)S(1)} %copy-done.1), kind=kOutput, calls=%fused_computation.1 | convolution fusion | flops 1358954496 | bytes 8257536 | tf_op jit(solution)/shard_map/dot_general | solution.py:39
  125.0 87.8 %all-reduce.1 = bf16[256,2304]{0,1:T(8,128)(2,1)S(1)} all-reduce(f32[256,2304]{0,1:T(8,128)} %convolution_bitcast_fusion), channel_id=1, replica_groups=mesh['dp'=8,'tensor'=4] {'tensor'}, use_global_device_ids=true, to_apply=%region_1.0 | all-reduce | flops 589824 | bytes 3538944 | tf_op jit(solution)/shard_map/psum | solution.py:16
  212.8 1.5 copy.12
Async XLA Ops:
  7.2 1.3 copy-start
  7.2 66.2 %reduce-scatter.2.cloned.1.call-start = ((), (), s32[]{:S(2)}) async-start(), calls=%async_computation.1 | async-start | bytes 5971968 | tf_op jit(solution)/shard_map/reduce_scatter | solution.py:26
  13.6 105.7 %all-gather.2.cloned.1.call-start = ((), (), s32[]{:S(2)}) async-start(), calls=%async_computation.2 | async-start | bytes 5971968 | tf_op jit(solution)/shard_map/all_gather | solution.py:41
  77.8 41.5 %copy-start.1 = (bf16[256,1152]{1,0:T(8,128)(2,1)S(1)}, bf16[256,1152]{1,0:T(8,128)(2,1)}, u32[]{:S(2)}) copy-start(bf16[256,1152]{1,0:T(8,128)(2,1)} %param.11) | copy-start | bytes 1769476
Sparse Core Ops, SparseCore 0:
  13.7 59.6 reduce-scatter.1
  77.9 41.3 all-gather.1
where the time goes:
time: 221 us
  waiting for transfers between devices  94.2 us (43%)
  blocking collectives  87.8 us (40%)
  matrix products  15.9 us (7%)
  between operations  14.1 us (6%)
  local copies, waits for them, and re-layouts  4.78 us (2%)
  other arithmetic  4.36 us (2%)
    psum x1, blocking collectives, tensor_total(): result = lax.psum(partial_value, 'tensor').astype(jnp.bfloat16)  87.8 us
    reduce_scatter x1, waiting for transfers between devices, shards(): lax.psum_scatter(lax.dot_general(out_grad, hidden, (((0,), (0,)), ((), ()...  57.7 us
    all_gather x1, waiting for transfers between devices, shards(): lax.all_gather(new_weight, 'dp', axis=0, tiled=True)  36.4 us
    dot_general x1, matrix products, shards(): lax.dot_general(next_hidden, lax.all_gather(new_weight, 'dp', axis=0, til...  5.68 us
    dot_general x1, matrix products, shards(): lax.dot_general(out_grad, hidden, (((0,), (0,)), ((), ())), preferred_ele...  5.12 us
    dot_general x1, matrix products, shards(): lax.dot_general(out_grad, weight, (((1,), (1,)), ((), ())), preferred_ele...  5.1 us
  transfers between devices with their start and end apart: 2, of which 2 were waited for; matrix products, arithmetic and copies ran while one was open for 3% of the time, Pallas kernels for 0%

commit v1 on v0

v1 whole, which is shorter than its diff:
```python
import functools

import jax
import jax.numpy as jnp
from jax import lax
from jax.experimental import pallas as pl
from jax.experimental.pallas import tpu as pltpu
from jax.sharding import PartitionSpec as P

MESH = pl.DeviceIdType.MESH

beta_first = 0.9
beta_second = 0.95
learn_rate = 0.001
weight_decay = 0.1
epsilon = 1e-08
correct_first = 0.999973438601112
correct_second = 0.99407947077967


def adam(first_moment, second_moment, grad):
    first_new = beta_first * first_moment + (1.0 - beta_first) * grad
    second_new = beta_second * second_moment + (1.0 - beta_second) * grad * grad
    return first_new, second_new


def kernel(
    n, m, chunks,
    og_t, hidden, out_grad_hbm, weight_hbm, current_hbm, first_hbm, second_hbm, next_hidden_hbm,
    grad_out, input_grad, new_weight, next_out,
    out_grad, weight, current, first, second, next_hidden,
    parts, whole, partial, inward, from_out, *rest,
):
    bits = n.bit_length() - 1
    landed = rest[:bits]
    (load_sem, rs_send, rs_recv, ag_send, ag_recv,
     in_send, a_recv, b_recv, out_send) = rest[bits:]
    half = m // 2
    rows = first.shape[0]
    rc = rows // chunks
    width = hidden.shape[1]
    me = lax.axis_index("dp")
    at = lax.axis_index("tensor")
    mine = [(me // (1 << b)) % 2 for b in range(bits)]
    partner = [me + (1 << b) * (1 - 2 * mine[b]) for b in range(bits)]
    left = at < half
    depth = jnp.where(left, half - 1 - at, at - half)
    inner = jnp.where(left, at + 1, at - 1)
    outer = jnp.where(left, at - 1, at + 1)
    has_outer = depth < half - 1

    loads = [
        pltpu.make_async_copy(src, dst, load_sem.at[i])
        for i, (src, dst) in enumerate((
            (first_hbm, first), (second_hbm, second), (current_hbm, current),
            (next_hidden_hbm, next_hidden), (out_grad_hbm, out_grad), (weight_hbm, weight),
        ))
    ]
    for load in loads:
        load.start()

    barrier = pltpu.get_barrier_semaphore()
    for b in range(bits):
        pl.semaphore_signal(barrier, inc=1, device_id={"dp": partner[b]}, device_id_type=MESH)
    pl.semaphore_signal(barrier, inc=1, device_id={"tensor": inner}, device_id_type=MESH)

    @pl.when(has_outer)
    def _():
        pl.semaphore_signal(barrier, inc=1, device_id={"tensor": outer}, device_id_type=MESH)

    pl.semaphore_wait(barrier, bits + 1 + jnp.where(has_outer, 1, 0))

    def order(c):
        high = list(range(1, bits))
        return [0] + (high if c % 2 == 0 else high[::-1])

    def region(c, fixed):
        return (c,) + tuple(fixed.get(b, slice(None)) for b in reversed(range(bits)))

    def rs_copy(c, k):
        o = order(c)
        fixed = {b: mine[b] for b in o[:k]}
        fixed[o[k]] = 1 - mine[o[k]]
        return pltpu.make_async_remote_copy(
            src_ref=parts.at[region(c, fixed)],
            dst_ref=landed[k].at[c],
            send_sem=rs_send.at[c, k],
            recv_sem=rs_recv.at[c, k],
            device_id={"dp": partner[o[k]]},
            device_id_type=MESH,
        )

    def ag_copy(c, j):
        o = order(c)
        k = bits - 1 - j
        fixed = {b: mine[b] for b in o[: k + 1]}
        return pltpu.make_async_remote_copy(
            src_ref=whole.at[region(c, fixed)],
            dst_ref=whole.at[region(c, fixed)],
            send_sem=ag_send.at[c, j],
            recv_sem=ag_recv.at[c, j],
            device_id={"dp": partner[o[k]]},
            device_id_type=MESH,
        )

    def in_copy(c, middle):
        return pltpu.make_async_remote_copy(
            src_ref=inward.at[c],
            dst_ref=(next_out if middle else from_out).at[c],
            send_sem=in_send.at[c],
            recv_sem=(b_recv if middle else a_recv).at[c],
            device_id={"tensor": inner},
            device_id_type=MESH,
        )

    def out_copy(c):
        return pltpu.make_async_remote_copy(
            src_ref=next_out.at[c],
            dst_ref=next_out.at[c],
            send_sem=out_send.at[c],
            recv_sem=b_recv.at[c],
            device_id={"tensor": outer},
            device_id_type=MESH,
        )

    def send_inward(c):
        if half == 1:
            in_copy(c, True).start()
        else:
            @pl.when(depth > 0)
            def _():
                in_copy(c, False).start()

            @pl.when(depth == 0)
            def _():
                in_copy(c, True).start()

    def stage(c, s):
        o = order(c)
        if s == 0:
            lhs = jnp.concatenate(
                [og_t[q * rows + c * rc : q * rows + (c + 1) * rc, :] for q in range(n)], axis=0
            )
            part = jnp.dot(lhs, hidden[...], preferred_element_type=jnp.float32)
            parts[c] = part.astype(jnp.bfloat16).reshape((2,) * bits + (rc, width))
            rs_copy(c, 0).start()
        elif s < bits:
            rs_copy(c, s - 1).wait_recv()
            keep = region(c, {b: mine[b] for b in o[:s]})
            parts[keep] = (
                parts[keep].astype(jnp.float32) + landed[s - 1][c].astype(jnp.float32)
            ).astype(jnp.bfloat16)
            rs_copy(c, s).start()
        elif s == bits:
            rs_copy(c, bits - 1).wait_recv()
            own = region(c, dict(enumerate(mine)))
            grad = (
                parts[own].astype(jnp.float32) + landed[bits - 1][c].astype(jnp.float32)
            ).astype(jnp.bfloat16)
            span = slice(c * rc, (c + 1) * rc)
            grad_out[span, :] = grad
            first_new, second_new = adam(first[span, :], second[span, :], grad.astype(jnp.float32))
            update = first_new * (1.0 / correct_first) / (
                jnp.sqrt(second_new * (1.0 / correct_second)) + epsilon
            )
            now = current[span, :].astype(jnp.float32)
            result = (now - learn_rate * (update + weight_decay * now)).astype(jnp.bfloat16)
            new_weight[span, :] = result
            whole[own] = result
            ag_copy(c, 0).start()
        elif s < 2 * bits:
            ag_copy(c, s - bits - 1).wait_recv()
            ag_copy(c, s - bits).start()
        elif s == 2 * bits:
            ag_copy(c, bits - 1).wait_recv()
            product = lax.dot_general(
                whole[c].reshape((n * rc, width)), next_hidden[...],
                (((1,), (1,)), ((), ())), preferred_element_type=jnp.float32,
            )
            partial[c] = product

            @pl.when(jnp.logical_not(has_outer))
            def _():
                inward[c] = product.astype(jnp.bfloat16)
                send_inward(c)
        elif s == 2 * bits + 1:
            @pl.when(has_outer)
            def _():
                in_copy(c, False).wait_recv()
                inward[c] = (partial[c] + from_out[c].astype(jnp.float32)).astype(jnp.bfloat16)
                send_inward(c)
        else:
            out_copy(c).wait_recv()

            @pl.when(depth == 0)
            def _():
                next_out[c] = (
                    inward[c].astype(jnp.float32) + next_out[c].astype(jnp.float32)
                ).astype(jnp.bfloat16)

            @pl.when(has_outer)
            def _():
                out_copy(c).start()

    pieces = 3
    cut = width // pieces
    last = 2 * bits + 2
    for t in range(chunks + last):
        for c in range(chunks):
            if 0 <= t - c <= last:
                if t - c == bits and c == 0:
                    for load in loads[:3]:
                        load.wait()
                if t - c == 2 * bits and c == 0:
                    loads[3].wait()
                stage(c, t - c)
        if 1 <= t <= pieces:
            if t == 1:
                loads[4].wait()
                loads[5].wait()
            span = slice((t - 1) * cut, t * cut)
            input_grad[:, span] = lax.dot_general(
                out_grad[...], weight[span, :], (((1,), (1,)), ((), ())),
                preferred_element_type=jnp.float32,
            ).astype(jnp.bfloat16)

    for c in range(chunks):
        for k in range(bits):
            rs_copy(c, k).wait_send()
            ag_copy(c, k).wait_send()
        in_copy(c, False).wait_send()

        @pl.when(has_outer)
        def _():
            out_copy(c).wait_send()


def solution(mesh):
    n, m = mesh.shape["dp"], mesh.shape["tensor"]
    bits = n.bit_length() - 1

    def shards(hidden, out_grad, weight, first_moment, second_moment, next_hidden):
        tokens, width = hidden.shape
        rows = first_moment.shape[0]
        features = out_grad.shape[1]
        rc = 48
        chunks = rows // rc
        cube = (2,) * bits
        position = lax.axis_index("dp") * rows
        current = lax.dynamic_slice_in_dim(weight, position, rows, 1).T
        vmem = pl.BlockSpec(memory_space=pltpu.VMEM)
        hbm = pl.BlockSpec(memory_space=pl.ANY)
        bf16, f32 = jnp.bfloat16, jnp.float32
        dma = pltpu.SemaphoreType.DMA
        grad, input_grad, new_weight, next_out = pl.pallas_call(
            functools.partial(kernel, n, m, chunks),
            out_shape=(
                jax.ShapeDtypeStruct((rows, width), bf16),
                jax.ShapeDtypeStruct((tokens, width), bf16),
                jax.ShapeDtypeStruct((rows, width), bf16),
                jax.ShapeDtypeStruct((chunks, n * rc, tokens), bf16),
            ),
            in_specs=[vmem] * 2 + [hbm] * 6,
            out_specs=[vmem] * 4,
            scratch_shapes=[
                pltpu.VMEM(out_grad.shape, bf16),
                pltpu.VMEM(weight.shape, bf16),
                pltpu.VMEM((rows, width), bf16),
                pltpu.VMEM((rows, width), f32),
                pltpu.VMEM((rows, width), f32),
                pltpu.VMEM(next_hidden.shape, bf16),
                pltpu.VMEM((chunks,) + cube + (rc, width), bf16),
                pltpu.VMEM((chunks,) + cube + (rc, width), bf16),
                pltpu.VMEM((chunks, n * rc, tokens), f32),
                pltpu.VMEM((chunks, n * rc, tokens), bf16),
                pltpu.VMEM((chunks, n * rc, tokens), bf16),
            ]
            + [
                pltpu.VMEM((chunks,) + (2,) * (bits - 1 - k) + (rc, width), bf16)
                for k in range(bits)
            ]
            + [
                dma((6,)),
                dma((chunks, bits)), dma((chunks, bits)),
                dma((chunks, bits)), dma((chunks, bits)),
                dma((chunks,)), dma((chunks,)), dma((chunks,)), dma((chunks,)),
            ],
            compiler_params=pltpu.CompilerParams(
                collective_id=0, has_side_effects=True, vmem_limit_bytes=56 * 1024 * 1024
            ),
            cost_estimate=pl.CostEstimate(
                flops=6 * tokens * width * features,
                bytes_accessed=16 * 1024 * 1024,
                transcendentals=rows * width,
            ),
        )(out_grad.T, hidden, out_grad, weight, current, first_moment, second_moment, next_hidden)
        first_new, second_new = adam(first_moment, second_moment, grad.astype(f32))
        next_out = (
            next_out.reshape(chunks, n, rc, tokens).transpose(3, 1, 0, 2).reshape(tokens, features)
        )
        return input_grad, first_new, second_new, new_weight, next_out

    placed = (
        P("dp", "tensor"),
        P("dp", None),
        P("tensor", None),
        P("dp", "tensor"),
        P("dp", "tensor"),
        P("dp", "tensor"),
    )
    return jax.shard_map(
        shards,
        mesh=mesh,
        in_specs=placed,
        out_specs=(
            P("dp", "tensor"),
            P("dp", "tensor"),
            P("dp", "tensor"),
            P("dp", "tensor"),
            P("dp", None),
        ),
        check_vma=False,
    )
```

time: 221 us -> 113 us (0.51)
  Pallas kernels: 0 us -> 99.3 us
  waiting for transfers between devices: 94.2 us -> 0 us
  blocking collectives: 87.8 us -> 0 us
  matrix products: 15.9 us -> 0 us
  between operations: 14.1 us -> 0.68 us
  local copies, waits for them, and re-layouts: 4.78 us -> 9.52 us
    pallas_call x0 -> x1, Pallas kernels: none -> 99.3 us  [shards(): pl.pallas_call(functools.partial(kernel, n, m, chunks), out_shape=(jax.Sh...]
    psum x1 -> x0, blocking collectives: 87.8 us -> none  [tensor_total(): result = lax.psum(partial_value, 'tensor').astype(jnp.bfloat16)]
    reduce_scatter x1 -> x0, waiting for transfers between devices: 57.7 us -> none  [shards(): lax.psum_scatter(lax.dot_general(out_grad, hidden, (((0,), (0,)), ((), ()...]
    all_gather x1 -> x0, waiting for transfers between devices: 36.4 us -> none  [shards(): lax.all_gather(new_weight, 'dp', axis=0, tiled=True)]
    dot_general x3 -> x0, matrix products: 15.9 us -> none  [the longest x1 5.68 us: shards(): lax.dot_general(next_hidden, lax.all_gather(new_weight, 'dp', axis=0, til...]
    convert_element_type x1 -> x0, other arithmetic: 4.36 us -> none  [shards(): (current - learn_rate * (update + weight_decay * current)).astype(jnp.bfl...]
    unnamed x6 -> x15, local copies, waits for them, and re-layouts: 3.14 us -> 6.41 us
    add x0 -> x1, other arithmetic: none -> 3.25 us  [adam(): second_new = beta_second * second_moment + (1.0 - beta_second) * grad * grad]
  transfers between devices with their start and end apart: 2 -> 0, of which waited for: 2 -> 0; matrix products, arithmetic and copies ran while one was open for 3% -> 0% of each run, Pallas kernels for 0% -> 0%
where the time goes in v1:
time: 113 us
  Pallas kernels  99.3 us (88%)
  local copies, waits for them, and re-layouts  9.52 us (8%)
  other arithmetic  3.25 us (3%)
    pallas_call x1, Pallas kernels, shards(): pl.pallas_call(functools.partial(kernel, n, m, chunks), out_shape=(jax.Sh...  99.3 us
    unnamed x15, local copies, waits for them, and re-layouts  6.41 us
    add x1, other arithmetic, adam(): second_new = beta_second * second_moment + (1.0 - beta_second) * grad * grad  3.25 us

profile of v1, /device:TPU:0, one launch (start us, length us, event | category | flops | bytes accessed | tf_op | source)
XLA Modules:
  0.0 112.8 jit_solution(14567078417307029263)
XLA Ops:
  0.6 0.0 copy-start.1
  0.6 1.7 %constant_dynamic-slice_fusion = bf16[1152,288]{1,0:T(8,128)(2,1)S(1)} fusion(bf16[1152,2304]{1,0:T(8,128)(2,1)} %weight_hbm.1, s32[]{:T(128)S(6)} %select_n.3), kind=kLoop, calls=%fused_computation.4 | loop fusion | bytes 1327108 | tf_op jit(solution)/shard_map/dynamic_slice | solution.py:250
  2.4 1.1 %copy.18 = bf16[1152,288]{0,1:T(8,128)(2,1)} copy(bf16[1152,288]{1,0:T(8,128)(2,1)S(1)} %constant_dynamic-slice_fusion) | data formatting | bytes 1327104
  3.5 0.0 copy-done.1
  3.5 1.4 %copy.14 = bf16[256,2304]{0,1:T(8,128)(2,1)} copy(bf16[256,2304]{1,0:T(8,128)(2,1)S(1)} %copy-done.1) | data formatting | bytes 2359296 | tf_op args[1]
  4.9 99.3 %shard_map.101 = (bf16[288,1152]{1,0:T(8,128)(2,1)}, bf16[256,1152]{1,0:T(8,128)(2,1)}, bf16[288,1152]{1,0:T(8,128)(2,1)}, bf16[6,384,256]{2,1,0:T(8,128)(2,1)}) custom-call(bf16[2304,256]{1,0:T(8,128)(2,1)} %bitcast.8, bf16[256,1152]{1,0:T(8,128)(2,1)} %hidden.1, bf16[256,2304]{1,0:T(8,128)(2,1)} %out_grad_hbm.1, bf16[1152,2304]{1,0:T(8,128)(2,1)} %weight_hbm.1, ...), custom_call_target="tpu_custom_call" | custom-call | flops 4076863488 | bytes 16777216 | tf_op jit(solution)/shard_map/pallas_call | solution.py:255
  104.3 1.4 %copy.16 = bf16[6,8,48,256]{3,2,0,1:T(8,128)(2,1)S(1)} copy(bf16[6,8,48,256]{3,2,1,0:T(8,128)(2,1)} %bitcast.7) | data formatting | bytes 2359296 | tf_op jit(solution)/shard_map/reshape | solution.py:299
  105.6 0.0 copy-start
  105.6 0.0 copy-start.2
  105.7 1.5 %copy.17 = bf16[256,2304]{1,0:T(8,128)(2,1)} copy(bf16[256,2304]{0,1:T(8,128)(2,1)S(1)} %bitcast.6) | data formatting | bytes 2359296
  107.2 0.0 copy-done
  107.2 0.2 copy-done.2
  107.4 0.0 copy-start.4
  107.4 3.3 %fusion.1 = (f32[288,1152]{1,0:T(8,128)}, f32[288,1152]{1,0:T(8,128)}) fusion(bf16[288,1152]{1,0:T(8,128)(2,1)S(1)} %copy-done.2, f32[288,1152]{1,0:T(8,128)} %second_hbm.1, f32[288,1152]{1,0:T(8,128)S(1)} %copy-done), kind=kLoop, calls=%fused_computation.3 | loop fusion | flops 2654208 | bytes 5971968 | tf_op jit(solution)/shard_map/add | solution.py:23
  110.6 0.0 copy-start.3
  110.6 0.0 copy-done.4
  110.6 0.8 copy.21
  111.4 0.5 copy-done.3
  111.9 0.8 copy.22
Async XLA Ops:
  0.6 2.9 %copy-start.1 = (bf16[256,2304]{1,0:T(8,128)(2,1)S(1)}, bf16[256,2304]{1,0:T(8,128)(2,1)}, u32[]{:S(2)}) copy-start(bf16[256,2304]{1,0:T(8,128)(2,1)} %out_grad_hbm.1) | copy-start | bytes 3538948
  105.6 1.6 %copy-start = (f32[288,1152]{1,0:T(8,128)S(1)}, f32[288,1152]{1,0:T(8,128)}, u32[]{:S(2)}) copy-start(f32[288,1152]{1,0:T(8,128)} %first_hbm.1) | copy-start | bytes 3981316
  105.6 1.7 %copy-start.2 = (bf16[288,1152]{1,0:T(8,128)(2,1)S(1)}, bf16[288,1152]{1,0:T(8,128)(2,1)}, u32[]{:S(2)}) copy-start(bf16[288,1152]{1,0:T(8,128)(2,1)} %get-tuple-element.10) | copy-start | bytes 1990660
  107.4 3.3 %copy-start.4 = (bf16[256,1152]{1,0:T(8,128)(2,1)S(1)}, bf16[256,1152]{1,0:T(8,128)(2,1)}, u32[]{:S(2)}) copy-start(bf16[256,1152]{1,0:T(8,128)(2,1)} %get-tuple-element.25) | copy-start | bytes 1769476
  110.6 1.3 %copy-start.3 = (bf16[288,1152]{1,0:T(8,128)(2,1)S(1)}, bf16[288,1152]{1,0:T(8,128)(2,1)}, u32[]{:S(2)}) copy-start(bf16[288,1152]{1,0:T(8,128)(2,1)} %get-tuple-element.28) | copy-start | bytes 1990660

commit v2 on v1

--- a/solution.py
+++ b/solution.py
@@ -1,4 +1,5 @@
 import functools
+import math
 
 import jax
 import jax.numpy as jnp
@@ -24,11 +25,15 @@
     return first_new, second_new
 
 
+def window_size(rows):
+    return -(-(rows + 128 - math.gcd(rows, 128)) // 128) * 128
+
+
 def kernel(
-    n, m, chunks,
-    og_t, hidden, out_grad_hbm, weight_hbm, current_hbm, first_hbm, second_hbm, next_hidden_hbm,
+    n, m, chunks, lag,
+    out_grad, hidden, weight_hbm, first_hbm, second_hbm, next_hidden_hbm,
     grad_out, input_grad, new_weight, next_out,
-    out_grad, weight, current, first, second, next_hidden,
+    og_t, weight, current, first, second, next_hidden,
     parts, whole, partial, inward, from_out, *rest,
 ):
     bits = n.bit_length() - 1
@@ -38,6 +43,7 @@
     half = m // 2
     rows = first.shape[0]
     rc = rows // chunks
+    group = 3 if chunks % 3 == 0 else 1
     width = hidden.shape[1]
     me = lax.axis_index("dp")
     at = lax.axis_index("tensor")
@@ -52,8 +58,8 @@
     loads = [
         pltpu.make_async_copy(src, dst, load_sem.at[i])
         for i, (src, dst) in enumerate((
-            (first_hbm, first), (second_hbm, second), (current_hbm, current),
-            (next_hidden_hbm, next_hidden), (out_grad_hbm, out_grad), (weight_hbm, weight),
+            (weight_hbm, weight), (first_hbm, first), (second_hbm, second),
+            (next_hidden_hbm, next_hidden),
         ))
     ]
     for load in loads:
@@ -68,6 +74,7 @@
     def _():
         pl.semaphore_signal(barrier, inc=1, device_id={"tensor": outer}, device_id_type=MESH)
 
+    og_t[...] = out_grad[...].T
     pl.semaphore_wait(barrier, bits + 1 + jnp.where(has_outer, 1, 0))
 
     def order(c):
@@ -106,7 +113,7 @@
     def in_copy(c, middle):
         return pltpu.make_async_remote_copy(
             src_ref=inward.at[c],
-            dst_ref=(next_out if middle else from_out).at[c],
+            dst_ref=next_out.at[:, c] if middle else from_out.at[c],
             send_sem=in_send.at[c],
             recv_sem=(b_recv if middle else a_recv).at[c],
             device_id={"tensor": inner},
@@ -115,8 +122,8 @@
 
     def out_copy(c):
         return pltpu.make_async_remote_copy(
-            src_ref=next_out.at[c],
-            dst_ref=next_out.at[c],
+            src_ref=next_out.at[:, c],
+            dst_ref=next_out.at[:, c],
             send_sem=out_send.at[c],
             recv_sem=b_recv.at[c],
             device_id={"tensor": outer},
@@ -138,11 +145,18 @@
     def stage(c, s):
         o = order(c)
         if s == 0:
-            lhs = jnp.concatenate(
-                [og_t[q * rows + c * rc : q * rows + (c + 1) * rc, :] for q in range(n)], axis=0
-            )
-            part = jnp.dot(lhs, hidden[...], preferred_element_type=jnp.float32)
-            parts[c] = part.astype(jnp.bfloat16).reshape((2,) * bits + (rc, width))
+            if c % group == 0:
+                lhs = jnp.concatenate(
+                    [
+                        og_t[q * rows + d * rc : q * rows + (d + 1) * rc, :]
+                        for d in range(c, c + group) for q in range(n)
+                    ],
+                    axis=0,
+                )
+                part = jnp.dot(lhs, hidden[...], preferred_element_type=jnp.float32)
+                parts[c : c + group] = part.astype(jnp.bfloat16).reshape(
+                    (group,) + (2,) * bits + (rc, width)
+                )
             rs_copy(c, 0).start()
         elif s < bits:
             rs_copy(c, s - 1).wait_recv()
@@ -163,7 +177,7 @@
             update = first_new * (1.0 / correct_first) / (
                 jnp.sqrt(second_new * (1.0 / correct_second)) + epsilon
             )
-            now = current[span, :].astype(jnp.float32)
+            now = current[span, :]
             result = (now - learn_rate * (update + weight_decay * now)).astype(jnp.bfloat16)
             new_weight[span, :] = result
             whole[own] = result
@@ -177,6 +191,7 @@
                 whole[c].reshape((n * rc, width)), next_hidden[...],
                 (((1,), (1,)), ((), ())), preferred_element_type=jnp.float32,
             )
+            product = product.reshape((n, rc, product.shape[1]))
             partial[c] = product
 
             @pl.when(jnp.logical_not(has_outer))
@@ -194,31 +209,44 @@
 
             @pl.when(depth == 0)
             def _():
-                next_out[c] = (
-                    inward[c].astype(jnp.float32) + next_out[c].astype(jnp.float32)
+                next_out[:, c] = (
+                    inward[c].astype(jnp.float32) + next_out[:, c].astype(jnp.float32)
                 ).astype(jnp.bfloat16)
 
             @pl.when(has_outer)
             def _():
                 out_copy(c).start()
+
+    def own_weight():
+        span = window_size(rows)
+        start = (me * rows) // 128 * 128
+        near = weight[:, pl.ds(pl.multiple_of(start, 128), span)]
+        shift = me * rows - start
+        row = lax.broadcasted_iota(jnp.int32, (rows, span), 0)
+        column = lax.broadcasted_iota(jnp.int32, (rows, span), 1)
+        pick = jnp.where(column == row + shift, 1.0, 0.0).astype(jnp.bfloat16)
+        current[...] = lax.dot_general(
+            pick, near, (((1,), (1,)), ((), ())), preferred_element_type=jnp.float32
+        )
 
     pieces = 3
     cut = width // pieces
     last = 2 * bits + 2
-    for t in range(chunks + last):
-        for c in range(chunks):
-            if 0 <= t - c <= last:
-                if t - c == bits and c == 0:
-                    for load in loads[:3]:
-                        load.wait()
-                if t - c == 2 * bits and c == 0:
+    for t in range(chunks + lag * last):
+        for s in reversed(range(last + 1)):
+            c = t - lag * s
+            if 0 <= c < chunks:
+                if s == bits and c == 0:
+                    loads[1].wait()
+                    loads[2].wait()
+                if s == 2 * bits and c == 0:
                     loads[3].wait()
-                stage(c, t - c)
-        if 1 <= t <= pieces:
-            if t == 1:
-                loads[4].wait()
-                loads[5].wait()
-            span = slice((t - 1) * cut, t * cut)
+                stage(c, s)
+        if t == 1:
+            loads[0].wait()
+            own_weight()
+        if t in (4, 6, 8):
+            span = slice((t - 4) // 2 * cut, (t - 2) // 2 * cut)
             input_grad[:, span] = lax.dot_general(
                 out_grad[...], weight[span, :], (((1,), (1,)), ((), ())),
                 preferred_element_type=jnp.float32,
@@ -243,44 +271,42 @@
         tokens, width = hidden.shape
         rows = first_moment.shape[0]
         features = out_grad.shape[1]
-        rc = 48
+        rc = 16
         chunks = rows // rc
         cube = (2,) * bits
-        position = lax.axis_index("dp") * rows
-        current = lax.dynamic_slice_in_dim(weight, position, rows, 1).T
         vmem = pl.BlockSpec(memory_space=pltpu.VMEM)
         hbm = pl.BlockSpec(memory_space=pl.ANY)
         bf16, f32 = jnp.bfloat16, jnp.float32
         dma = pltpu.SemaphoreType.DMA
         grad, input_grad, new_weight, next_out = pl.pallas_call(
-            functools.partial(kernel, n, m, chunks),
+            functools.partial(kernel, n, m, chunks, 3),
             out_shape=(
                 jax.ShapeDtypeStruct((rows, width), bf16),
                 jax.ShapeDtypeStruct((tokens, width), bf16),
                 jax.ShapeDtypeStruct((rows, width), bf16),
-                jax.ShapeDtypeStruct((chunks, n * rc, tokens), bf16),
+                jax.ShapeDtypeStruct((n, chunks, rc, tokens), bf16),
             ),
-            in_specs=[vmem] * 2 + [hbm] * 6,
+            in_specs=[vmem] * 2 + [hbm] * 4,
             out_specs=[vmem] * 4,
             scratch_shapes=[
-                pltpu.VMEM(out_grad.shape, bf16),
+                pltpu.VMEM((features, tokens), bf16),
                 pltpu.VMEM(weight.shape, bf16),
-                pltpu.VMEM((rows, width), bf16),
+                pltpu.VMEM((rows, width), f32),
                 pltpu.VMEM((rows, width), f32),
                 pltpu.VMEM((rows, width), f32),
                 pltpu.VMEM(next_hidden.shape, bf16),
                 pltpu.VMEM((chunks,) + cube + (rc, width), bf16),
                 pltpu.VMEM((chunks,) + cube + (rc, width), bf16),
-                pltpu.VMEM((chunks, n * rc, tokens), f32),
-                pltpu.VMEM((chunks, n * rc, tokens), bf16),
-                pltpu.VMEM((chunks, n * rc, tokens), bf16),
+                pltpu.VMEM((chunks, n, rc, tokens), f32),
+                pltpu.VMEM((chunks, n, rc, tokens), bf16),
+                pltpu.VMEM((chunks, n, rc, tokens), bf16),
             ]
             + [
                 pltpu.VMEM((chunks,) + (2,) * (bits - 1 - k) + (rc, width), bf16)
                 for k in range(bits)
             ]
             + [
-                dma((6,)),
+                dma((4,)),
                 dma((chunks, bits)), dma((chunks, bits)),
                 dma((chunks, bits)), dma((chunks, bits)),
                 dma((chunks,)), dma((chunks,)), dma((chunks,)), dma((chunks,)),
@@ -293,11 +319,9 @@
                 bytes_accessed=16 * 1024 * 1024,
                 transcendentals=rows * width,
             ),
-        )(out_grad.T, hidden, out_grad, weight, current, first_moment, second_moment, next_hidden)
+        )(out_grad, hidden, weight, first_moment, second_moment, next_hidden)
         first_new, second_new = adam(first_moment, second_moment, grad.astype(f32))
-        next_out = (
-            next_out.reshape(chunks, n, rc, tokens).transpose(3, 1, 0, 2).reshape(tokens, features)
-        )
+        next_out = next_out.reshape(features, tokens).T
         return input_grad, first_new, second_new, new_weight, next_out
 
     placed = (

time: 113 us -> 92.7 us (0.82)
  Pallas kernels: 99.3 us -> 85.3 us
  local copies, waits for them, and re-layouts: 9.52 us -> 4.67 us
  other arithmetic: 3.25 us -> 1.87 us
    pallas_call x1, Pallas kernels: 99.3 us -> 85.3 us  [shards(): pl.pallas_call(functools.partial(kernel, n, m, chunks, 3), out_shape=(jax...]
    unnamed x15 -> x12, local copies, waits for them, and re-layouts: 6.41 us -> 2.16 us
    dynamic_slice x1 -> x0, local copies, waits for them, and re-layouts: 1.74 us -> none  [shards(): current = lax.dynamic_slice_in_dim(weight, position, rows, 1).T]
    add x1, other arithmetic: 3.25 us -> 1.87 us  [adam(): second_new = beta_second * second_moment + (1.0 - beta_second) * grad * grad]
    reshape x1, local copies, waits for them, and re-layouts: 1.37 us -> 2.52 us  [shards(): next_out = next_out.reshape(features, tokens).T]
where the time goes in v2:
time: 92.7 us; the launch traced here: 92.5 us
  Pallas kernels  85.3 us (92%)
  local copies, waits for them, and re-layouts  4.67 us (5%)
  other arithmetic  1.87 us (2%)
    pallas_call x1, Pallas kernels, shards(): pl.pallas_call(functools.partial(kernel, n, m, chunks, 3), out_shape=(jax...  85.3 us
    reshape x1, local copies, waits for them, and re-layouts, shards(): next_out = next_out.reshape(features, tokens).T  2.52 us
    unnamed x12, local copies, waits for them, and re-layouts  2.16 us
    add x1, other arithmetic, adam(): second_new = beta_second * second_moment + (1.0 - beta_second) * grad * grad  1.87 us

profile of v2, /device:TPU:0, one launch (start us, length us, event | category | flops | bytes accessed | tf_op | source)
XLA Modules:
  0.0 92.5 jit_solution(10092163975441323496)
XLA Ops:
  0.6 0.0 copy-start.1
  0.6 85.3 %shard_map.101 = (bf16[288,1152]{1,0:T(8,128)(2,1)}, bf16[256,1152]{1,0:T(8,128)(2,1)}, bf16[288,1152]{1,0:T(8,128)(2,1)}, bf16[8,18,16,256]{3,2,1,0:T(8,128)(2,1)}) custom-call(bf16[256,2304]{1,0:T(8,128)(2,1)} %out_grad.1, bf16[256,1152]{1,0:T(8,128)(2,1)} %hidden.1, bf16[1152,2304]{1,0:T(8,128)(2,1)} %weight_hbm.1, f32[288,1152]{1,0:T(8,128)} %first_hbm.1, ...), custom_call_target="tpu_custom_call" | custom-call | flops 4076863488 | bytes 16777216 | tf_op jit(solution)/shard_map/pallas_call | solution.py:281
  85.9 0.0 copy-start
  85.9 0.0 copy-start.2
  85.9 2.5 %copy.11 = bf16[2304,256]{0,1:T(8,128)(2,1)} copy(bf16[2304,256]{1,0:T(8,128)(2,1)} %bitcast.3) | data formatting | bytes 2359296 | tf_op jit(solution)/shard_map/reshape | solution.py:324
  88.5 0.0 copy-done.1
  88.5 0.0 copy-done
  88.5 0.0 copy-done.2
  88.5 0.0 copy-start.4
  88.5 1.9 %fusion.1 = (f32[288,1152]{1,0:T(8,128)}, f32[288,1152]{1,0:T(8,128)}) fusion(bf16[288,1152]{1,0:T(8,128)(2,1)S(1)} %copy-done.2, f32[288,1152]{1,0:T(8,128)S(1)} %copy-done.1, f32[288,1152]{1,0:T(8,128)S(1)} %copy-done), kind=kLoop, calls=%fused_computation.3 | loop fusion | flops 2654208 | bytes 5971968 | tf_op jit(solution)/shard_map/add | solution.py:24
  90.4 0.0 copy-start.3
  90.4 0.0 copy-done.4
  90.4 0.8 copy.14
  91.2 0.5 copy-done.3
  91.7 0.8 copy.15
Async XLA Ops:
  0.6 87.8 %copy-start.1 = (f32[288,1152]{1,0:T(8,128)S(1)}, f32[288,1152]{1,0:T(8,128)}, u32[]{:S(2)}) copy-start(f32[288,1152]{1,0:T(8,128)} %second_hbm.1) | copy-start | bytes 3981316
  85.9 2.5 %copy-start = (f32[288,1152]{1,0:T(8,128)S(1)}, f32[288,1152]{1,0:T(8,128)}, u32[]{:S(2)}) copy-start(f32[288,1152]{1,0:T(8,128)} %first_hbm.1) | copy-start | bytes 3981316
  85.9 2.5 %copy-start.2 = (bf16[288,1152]{1,0:T(8,128)(2,1)S(1)}, bf16[288,1152]{1,0:T(8,128)(2,1)}, u32[]{:S(2)}) copy-start(bf16[288,1152]{1,0:T(8,128)(2,1)} %get-tuple-element.10) | copy-start | bytes 1990660
  88.5 1.9 %copy-start.4 = (bf16[256,1152]{1,0:T(8,128)(2,1)S(1)}, bf16[256,1152]{1,0:T(8,128)(2,1)}, u32[]{:S(2)}) copy-start(bf16[256,1152]{1,0:T(8,128)(2,1)} %get-tuple-element.20) | copy-start | bytes 1769476
  90.4 1.3 %copy-start.3 = (bf16[288,1152]{1,0:T(8,128)(2,1)S(1)}, bf16[288,1152]{1,0:T(8,128)(2,1)}, u32[]{:S(2)}) copy-start(bf16[288,1152]{1,0:T(8,128)(2,1)} %get-tuple-element.23) | copy-start | bytes 1990660

commit v3 on v2

--- a/solution.py
+++ b/solution.py
@@ -33,7 +33,7 @@
     n, m, chunks, lag,
     out_grad, hidden, weight_hbm, first_hbm, second_hbm, next_hidden_hbm,
     grad_out, input_grad, new_weight, next_out,
-    og_t, weight, current, first, second, next_hidden,
+    og_t, weight, current, first, second, next_hidden, next_t,
     parts, whole, partial, inward, from_out, *rest,
 ):
     bits = n.bit_length() - 1
@@ -161,9 +161,7 @@
         elif s < bits:
             rs_copy(c, s - 1).wait_recv()
             keep = region(c, {b: mine[b] for b in o[:s]})
-            parts[keep] = (
-                parts[keep].astype(jnp.float32) + landed[s - 1][c].astype(jnp.float32)
-            ).astype(jnp.bfloat16)
+            parts[keep] = parts[keep] + landed[s - 1][c]
             rs_copy(c, s).start()
         elif s == bits:
             rs_copy(c, bits - 1).wait_recv()
@@ -187,9 +185,9 @@
             ag_copy(c, s - bits).start()
         elif s == 2 * bits:
             ag_copy(c, bits - 1).wait_recv()
-            product = lax.dot_general(
-                whole[c].reshape((n * rc, width)), next_hidden[...],
-                (((1,), (1,)), ((), ())), preferred_element_type=jnp.float32,
+            product = jnp.dot(
+                whole[c].reshape((n * rc, width)), next_t[...],
+                preferred_element_type=jnp.float32,
             )
             product = product.reshape((n, rc, product.shape[1]))
             partial[c] = product
@@ -239,12 +237,13 @@
                 if s == bits and c == 0:
                     loads[1].wait()
                     loads[2].wait()
-                if s == 2 * bits and c == 0:
-                    loads[3].wait()
                 stage(c, s)
         if t == 1:
             loads[0].wait()
             own_weight()
+        if t == 2:
+            loads[3].wait()
+            next_t[...] = next_hidden[...].T
         if t in (4, 6, 8):
             span = slice((t - 4) // 2 * cut, (t - 2) // 2 * cut)
             input_grad[:, span] = lax.dot_general(
@@ -295,6 +294,7 @@
                 pltpu.VMEM((rows, width), f32),
                 pltpu.VMEM((rows, width), f32),
                 pltpu.VMEM(next_hidden.shape, bf16),
+                pltpu.VMEM((width, tokens), bf16),
                 pltpu.VMEM((chunks,) + cube + (rc, width), bf16),
                 pltpu.VMEM((chunks,) + cube + (rc, width), bf16),
                 pltpu.VMEM((chunks, n, rc, tokens), f32),

time: 92.7 us -> 91.9 us (level)
  no operation moved by 1% of the time
where the time goes in v3:
time: 91.9 us; the launch traced here: 91.7 us
  Pallas kernels  84.5 us (92%)
  local copies, waits for them, and re-layouts  4.67 us (5%)
  other arithmetic  1.87 us (2%)
    pallas_call x1, Pallas kernels, shards(): pl.pallas_call(functools.partial(kernel, n, m, chunks, 3), out_shape=(jax...  84.5 us
    reshape x1, local copies, waits for them, and re-layouts, shards(): next_out = next_out.reshape(features, tokens).T  2.52 us
    unnamed x12, local copies, waits for them, and re-layouts  2.16 us
    add x1, other arithmetic, adam(): second_new = beta_second * second_moment + (1.0 - beta_second) * grad * grad  1.87 us

profile of v3, /device:TPU:0, one launch (start us, length us, event | category | flops | bytes accessed | tf_op | source)
XLA Modules:
  0.0 91.7 jit_solution(13240909975083721920)
XLA Ops:
  0.6 0.0 copy-start.1
  0.6 84.5 %shard_map.101 = (bf16[288,1152]{1,0:T(8,128)(2,1)}, bf16[256,1152]{1,0:T(8,128)(2,1)}, bf16[288,1152]{1,0:T(8,128)(2,1)}, bf16[8,18,16,256]{3,2,1,0:T(8,128)(2,1)}) custom-call(bf16[256,2304]{1,0:T(8,128)(2,1)} %out_grad.1, bf16[256,1152]{1,0:T(8,128)(2,1)} %hidden.1, bf16[1152,2304]{1,0:T(8,128)(2,1)} %weight_hbm.1, f32[288,1152]{1,0:T(8,128)} %first_hbm.1, ...), custom_call_target="tpu_custom_call" | custom-call | flops 4076863488 | bytes 16777216 | tf_op jit(solution)/shard_map/pallas_call | solution.py:280
  85.2 0.0 copy-start
  85.2 0.0 copy-start.2
  85.2 2.5 %copy.11 = bf16[2304,256]{0,1:T(8,128)(2,1)} copy(bf16[2304,256]{1,0:T(8,128)(2,1)} %bitcast.3) | data formatting | bytes 2359296 | tf_op jit(solution)/shard_map/reshape | solution.py:324
  87.7 0.0 copy-done.1
  87.7 0.0 copy-done
  87.7 0.0 copy-done.2
  87.7 0.0 copy-start.4
  87.7 1.9 %fusion.1 = (f32[288,1152]{1,0:T(8,128)}, f32[288,1152]{1,0:T(8,128)}) fusion(bf16[288,1152]{1,0:T(8,128)(2,1)S(1)} %copy-done.2, f32[288,1152]{1,0:T(8,128)S(1)} %copy-done.1, f32[288,1152]{1,0:T(8,128)S(1)} %copy-done), kind=kLoop, calls=%fused_computation.3 | loop fusion | flops 2654208 | bytes 5971968 | tf_op jit(solution)/shard_map/add | solution.py:24
  89.6 0.0 copy-start.3
  89.6 0.0 copy-done.4
  89.6 0.8 copy.14
  90.4 0.5 copy-done.3
  90.9 0.8 copy.15
Async XLA Ops:
  0.6 87.1 %copy-start.1 = (f32[288,1152]{1,0:T(8,128)S(1)}, f32[288,1152]{1,0:T(8,128)}, u32[]{:S(2)}) copy-start(f32[288,1152]{1,0:T(8,128)} %second_hbm.1) | copy-start | bytes 3981316
  85.2 2.5 %copy-start = (f32[288,1152]{1,0:T(8,128)S(1)}, f32[288,1152]{1,0:T(8,128)}, u32[]{:S(2)}) copy-start(f32[288,1152]{1,0:T(8,128)} %first_hbm.1) | copy-start | bytes 3981316
  85.2 2.5 %copy-start.2 = (bf16[288,1152]{1,0:T(8,128)(2,1)S(1)}, bf16[288,1152]{1,0:T(8,128)(2,1)}, u32[]{:S(2)}) copy-start(bf16[288,1152]{1,0:T(8,128)(2,1)} %get-tuple-element.10) | copy-start | bytes 1990660
  87.7 1.9 %copy-start.4 = (bf16[256,1152]{1,0:T(8,128)(2,1)S(1)}, bf16[256,1152]{1,0:T(8,128)(2,1)}, u32[]{:S(2)}) copy-start(bf16[256,1152]{1,0:T(8,128)(2,1)} %get-tuple-element.20) | copy-start | bytes 1769476
  89.6 1.3 %copy-start.3 = (bf16[288,1152]{1,0:T(8,128)(2,1)S(1)}, bf16[288,1152]{1,0:T(8,128)(2,1)}, u32[]{:S(2)}) copy-start(bf16[288,1152]{1,0:T(8,128)(2,1)} %get-tuple-element.23) | copy-start | bytes 1990660
